TPU v7x, 32 devices: a whole 2x2x4 slice. The times are simulated.
32 devices in a mesh: psg: 32 (over z, y, x, core), qry: 1.
Axes of the slice: x: 2, y: 2, z: 4, core: 2. Of those that a mesh axis runs over, the one named last changes fastest.
Arguments:
- queries: bfloat16 [1024, 4096], P('psg', 'qry'), may hold values from -6 to 6
- grad_out: bfloat16 [1024, 4096], P('psg', 'qry'), may hold values from -6 to 6
- attn_out: bfloat16 [1024, 4096], P('psg', 'qry'), may hold values from -6 to 6
- log_sum: float32 [32, 1024], P('qry', 'psg'), may hold values from 3 to 5
- keys: bfloat16 [16384, 1024], P('psg', 'qry'), may hold values from -6 to 6
- values: bfloat16 [16384, 1024], P('psg', 'qry'), may hold values from -6 to 6
- proj_weight: bfloat16 [4096, 4096], P('psg', 'qry'), may hold values from -0.09375 to 0.09375
- attend: int32 [4, 16], replicated, may hold values from 0 to 31, all different within a row; in each aligned block of 4 rows (0 to 3, 4 to 7, ...) at most 4 rows name the same one
- qlen: int32 [4], replicated, may hold values from 128 to 256, as said below
Outputs:
- grad_query: float32 [1024, 4096], P('psg', 'qry')
- grad_keys: float32 [16384, 1024], P('psg', 'qry')
- grad_values: float32 [16384, 1024], P('psg', 'qry')
- grad_hidden: float32 [1024, 4096], P('psg')
Inputs may be any that keep to these rules, and one draw needn't show every extreme that they name: `attend`: each question names 16 different blocks; each block is named by at least one question and at most 4, and some block by exactly 4. `qlen`: each a multiple of 128; some question has 256 rows.
All inputs are finite; a program needn't handle non-finite values.
Results may differ from a plain program's by a relative error of at most 0.0049.
Values may be sent and summed in bfloat16 or wider, within the bound.
A program may use at most 128 MiB of HBM per device.

v0:
```python
import jax
import jax.numpy as jnp
from jax import lax
from jax.sharding import PartitionSpec as P

ATTN_WIDTH = 128
GROUP = 4
PADDED_ASK_LEN = 256
TOPB = 16


def row_delta(grad_out, attn_out, head_count):
    products = grad_out.astype(jnp.float32) * attn_out.astype(jnp.float32)
    return jnp.sum(products.reshape(products.shape[0], head_count, ATTN_WIDTH), axis=2).T


def on_device(queries, grad_out, attn_out, log_sum, keys, values, proj_weight, attend, qlen):
    inverse_root_dimension = ATTN_WIDTH ** (-0.5)
    row_count, number_of_columns = queries.shape
    head_count = log_sum.shape[0]
    kv_local = head_count // GROUP
    block_len = keys.shape[0]
    psg_count = lax.axis_size("psg")
    owner_block = lax.axis_index("psg")
    all_queries, all_grads, all_outputs = (
        lax.all_gather(queries, "psg", axis=0, tiled=True),
        lax.all_gather(grad_out, "psg", axis=0, tiled=True),
        lax.all_gather(attn_out, "psg", axis=0, tiled=True),
    )
    all_lse = lax.all_gather(log_sum, "psg", axis=1, tiled=True)
    all_delta = row_delta(all_grads, all_outputs, head_count)
    total_rows = all_queries.shape[0]
    question_total = attend.shape[0]
    attending = jnp.any(attend == owner_block, axis=1).astype(jnp.int32)
    slot_total = jnp.sum(attending)
    slot_rank = jnp.cumsum(attending) - 1
    question_ids = jnp.arange(question_total, dtype=jnp.int32)
    capacity = min(question_total, 2 * question_total * TOPB // psg_count)
    slot_matrix = (attending[None, :] == 1) & (
        slot_rank[None, :] == jnp.arange(capacity, dtype=jnp.int32)[:, None]
    )
    slot_question = jnp.sum(jnp.where(slot_matrix, question_ids[None, :], 0), axis=1)
    passage_lookup_matrix = keys.reshape(block_len, kv_local, ATTN_WIDTH)
    value_block_rows = values.reshape(block_len, kv_local, ATTN_WIDTH)
    sub_len = min(512, block_len)
    sub_count = block_len // sub_len

    def visit(slot_index, totals):
        grad_q, grad_k, grad_v = totals
        question = slot_question[slot_index]
        row_start = question * PADDED_ASK_LEN
        asking_matrix_tile = lax.dynamic_slice_in_dim(
            all_queries, row_start, PADDED_ASK_LEN, 0
        ).reshape(PADDED_ASK_LEN, kv_local, GROUP, ATTN_WIDTH)
        output_gradient_rows = lax.dynamic_slice_in_dim(
            all_grads, row_start, PADDED_ASK_LEN, 0
        ).reshape(PADDED_ASK_LEN, kv_local, GROUP, ATTN_WIDTH)
        lse_rows = lax.dynamic_slice_in_dim(all_lse, row_start, PADDED_ASK_LEN, 1).reshape(
            kv_local, GROUP, PADDED_ASK_LEN
        )
        delta_rows = lax.dynamic_slice_in_dim(all_delta, row_start, PADDED_ASK_LEN, 1).reshape(
            kv_local, GROUP, PADDED_ASK_LEN
        )
        row_valid = (jnp.arange(PADDED_ASK_LEN) < qlen[question]).astype(jnp.float32)

        def sub_visit(sub_index, inner):
            inner_k, inner_v, query_acc = inner
            raw_attention_energies = (
                jnp.einsum(
                    "dlyb,ilb->lydi",
                    asking_matrix_tile,
                    passage_lookup_matrix,
                    preferred_element_type=jnp.float32,
                )
                * inverse_root_dimension
            )
            probs = (
                jnp.exp(raw_attention_energies - lse_rows[..., None])
                * row_valid[None, None, :, None]
            )
            probability_narrow = probs.astype(jnp.bfloat16)
            probability_gradient = jnp.einsum(
                "dlyb,ilb->lydi",
                output_gradient_rows,
                value_block_rows,
                preferred_element_type=jnp.float32,
            )
            energy_derivative_lowprec = (
                probs * (probability_gradient - delta_rows[..., None])
            ).astype(jnp.bfloat16)
            asking_partial_term = jnp.einsum(
                "ilgy,yiu->gilu",
                energy_derivative_lowprec,
                passage_lookup_matrix,
                preferred_element_type=jnp.float32,
            )
            lookup_partial_term = (
                jnp.einsum(
                    "nwde,dnwj->enj",
                    energy_derivative_lowprec,
                    asking_matrix_tile,
                    preferred_element_type=jnp.float32,
                )
                * inverse_root_dimension
            )
            value_contribution = jnp.einsum(
                "nwde,dnwj->enj",
                probability_narrow,
                output_gradient_rows,
                preferred_element_type=jnp.float32,
            )
            old_k = inner_k
            old_v = inner_v
            inner_k = old_k + lookup_partial_term.reshape(sub_len, kv_local * ATTN_WIDTH)
            inner_v = old_v + value_contribution.reshape(sub_len, kv_local * ATTN_WIDTH)
            return (inner_k, inner_v, query_acc + asking_partial_term)

        query_start = jnp.zeros((PADDED_ASK_LEN, kv_local, GROUP, ATTN_WIDTH), jnp.float32)
        grad_k, grad_v, asking_accumulator = lax.fori_loop(
            0, sub_count, sub_visit, (grad_k, grad_v, query_start)
        )
        grad_q = lax.dynamic_update_slice_in_dim(
            grad_q,
            (asking_accumulator * inverse_root_dimension).reshape(
                PADDED_ASK_LEN, number_of_columns
            ),
            row_start,
            0,
        )
        return (grad_q, grad_k, grad_v)

    start_totals = (
        jnp.zeros((total_rows, number_of_columns), jnp.float32),
        jnp.zeros((block_len, kv_local * ATTN_WIDTH), jnp.float32),
        jnp.zeros((block_len, kv_local * ATTN_WIDTH), jnp.float32),
    )
    query_terms, grad_keys, grad_values = lax.fori_loop(0, slot_total, visit, start_totals)
    grad_query = lax.psum_scatter(query_terms, "psg", scatter_dimension=0, tiled=True)
    query_low = grad_query.astype(jnp.bfloat16)
    hidden_terms = lax.dot_general(
        query_low,
        lax.all_gather(proj_weight, "psg", axis=0, tiled=True),
        (((1,), (1,)), ((), ())),
        preferred_element_type=jnp.float32,
    )
    grad_hidden = lax.psum(hidden_terms, "qry")
    return (grad_query, grad_keys, grad_values, grad_hidden)


def solution(mesh):
    in_specs = (
        P("psg", "qry"),
        P("psg", "qry"),
        P("psg", "qry"),
        P("qry", "psg"),
        P("psg", "qry"),
        P("psg", "qry"),
        P("psg", "qry"),
        P(),
        P(),
    )
    out_specs = (P("psg", "qry"), P("psg", "qry"), P("psg", "qry"), P("psg", None))
    return jax.shard_map(
        on_device, mesh=mesh, in_specs=in_specs, out_specs=out_specs, check_vma=False
    )
```

profile of v0, /device:TPU:0, one launch (start us, length us, event | category | flops | bytes accessed | tf_op | source)
XLA Modules:
  0.0 930.8 jit_solution(18242795014202352193)
XLA Ops:
  16.3 45.4 %all_gather.16 = f32[32,1024]{0,1:T(8,128)S(1)} all-gather(f32[32,32]{0,1:T(8,128)S(1)} %copy.63), channel_id=1, replica_groups=mesh['psg'=32,'qry'=1] {'psg'}, dimensions={1}, use_global_device_ids=true | all-gather | bytes 135168 | tf_op jit(solution)/shard_map/all_gather | solution.py:30
  62.6 29.7 %all-gather.7.cloned.1.call-done = bf16[1024,4096]{1,0:T(8,128)(2,1)} async-done(((bf16[32,4096]{1,0:T(8,128)(2,1)}), bf16[1024,4096]{1,0:T(8,128)(2,1)}) %all-gather.7.cloned.1.call-update) | async-done | bytes 8388624 | tf_op jit(solution)/shard_map/all_gather | solution.py:27
  92.3 78.9 %all-gather.9.cloned.1.call-done = bf16[1024,4096]{1,0:T(8,128)(2,1)} async-done(((bf16[32,4096]{1,0:T(8,128)(2,1)}), bf16[1024,4096]{1,0:T(8,128)(2,1)}) %all-gather.9.cloned.1.call-update) | async-done | bytes 8388624 | tf_op jit(solution)/shard_map/all_gather | solution.py:28
  171.3 7.4 multiply_bitcast_fusion
  178.6 7.0 copy.87
  185.6 8.3 reduce_sum.29
  194.1 56.1 %all-gather.5.cloned.1.call-done = bf16[1024,4096]{1,0:T(8,128)(2,1)} async-done(((bf16[32,4096]{1,0:T(8,128)(2,1)}), bf16[1024,4096]{1,0:T(8,128)(2,1)}) %all-gather.5.cloned.1.call-update) | async-done | bytes 8388624 | tf_op jit(solution)/shard_map/all_gather | solution.py:26
  250.2 7.8 broadcast_in_dim.21.clone
  261.2 133.9 %while.16 = (s32[]{:T(128)}, f32[1024,4096]{1,0:T(8,128)}, f32[512,1024]{0,1:T(8,128)}, f32[512,1024]{0,1:T(8,128)}, s32[]{:T(128)}, /*index=5*/s32[4]{0:T(128)S...) while((s32[]{:T(128)}, f32[1024,4096]{1,0:T(8,128)}, ...), condition=%wide.region_6.7_spmd, body=%wide.region_5.6_spmd.sunk | while | flops 5413274112 | bytes 188059136 | solution.py:137
  269.7 9.3 %fusion.45 = f32[8,256,4,512]{3,1,2,0:T(8,128)} fusion(bf16[256,8,4,128]{0,3,2,1:T(8,128)(2,1)S(1)} %bitcast.108, bf16[512,8,128]{0,2,1:T(8,128)(2,1)} %get-tuple-element.366), kind=kOutput, calls=%fused_computation.13.clone.1 | convolution fusion | flops 1073741824 | bytes 19922944 | tf_op jit(solution)/shard_map/while/body/while/body/eval_jaxpr/dlyb,ilb->lydi/dot_general | solution.py:69
  289.4 9.6 %fusion.46 = bf16[8,4,256,512]{3,2,1,0:T(8,128)(2,1)S(1)} fusion(f32[8,256,4,512]{3,1,2,0:T(8,128)} %fusion.45, bf16[256,8,4,128]{0,3,2,1:T(8,128)(2,1)} %bitcast.113, f32[8,4,256]{2,1,0:T(4,128)S(1)} %sub.75, f32[256]{0:T(256)S(1)} %compare_convert_fusion.2, f32[8,4,256]{2,1,0:T(4,128)S(1)} %sub.76, bf16[512,8,128]{2,0,1:T(8,128)(2,1)} %get-tuple-element.370), kind=kOutput, calls=%fused_computation.2.clone.1 | convolution fusion | flops 1098907648 | bytes 28378112 | tf_op jit(solution)/shard_map/while/body/while/body/eval_jaxpr/dlyb,ilb->lydi/dot_general | solution.py:82
  300.7 8.5 fusion.47
  312.9 4.8 convolution_multiply_fusion.2
  317.7 5.7 copy.93
  323.4 4.6 constant_dynamic-update-slice_fusion.2
  336.3 9.3 %fusion.45 = f32[8,256,4,512]{3,1,2,0:T(8,128)} fusion(bf16[256,8,4,128]{0,3,2,1:T(8,128)(2,1)S(1)} %bitcast.108, bf16[512,8,128]{0,2,1:T(8,128)(2,1)} %get-tuple-element.366), kind=kOutput, calls=%fused_computation.13.clone.1 | convolution fusion | flops 1073741824 | bytes 19922944 | tf_op jit(solution)/shard_map/while/body/while/body/eval_jaxpr/dlyb,ilb->lydi/dot_general | solution.py:69
  356.0 9.6 %fusion.46 = bf16[8,4,256,512]{3,2,1,0:T(8,128)(2,1)S(1)} fusion(f32[8,256,4,512]{3,1,2,0:T(8,128)} %fusion.45, bf16[256,8,4,128]{0,3,2,1:T(8,128)(2,1)} %bitcast.113, f32[8,4,256]{2,1,0:T(4,128)S(1)} %sub.75, f32[256]{0:T(256)S(1)} %compare_convert_fusion.2, f32[8,4,256]{2,1,0:T(4,128)S(1)} %sub.76, bf16[512,8,128]{2,0,1:T(8,128)(2,1)} %get-tuple-element.370), kind=kOutput, calls=%fused_computation.2.clone.1 | convolution fusion | flops 1098907648 | bytes 28378112 | tf_op jit(solution)/shard_map/while/body/while/body/eval_jaxpr/dlyb,ilb->lydi/dot_general | solution.py:82
  367.2 8.5 fusion.47
  379.5 4.8 convolution_multiply_fusion.2
  384.3 5.7 copy.93
  390.0 4.6 constant_dynamic-update-slice_fusion.2
  401.5 307.6 %reduce-scatter.2.cloned.1.call-done = f32[32,4096]{1,0:T(8,128)} async-done(((f32[1024,4096]{1,0:T(8,128)}), f32[32,4096]{1,0:T(8,128)}) %reduce-scatter.2.cloned.1.call-update) | async-done | bytes 524304 | tf_op jit(solution)/shard_map/reduce_scatter | solution.py:138
  709.0 199.2 %all-gather.11.cloned.1.call-done = bf16[4096,4096]{1,0:T(8,128)(2,1)} async-done(((bf16[128,4096]{1,0:T(8,128)(2,1)}), bf16[4096,4096]{1,0:T(8,128)(2,1)}) %all-gather.11.cloned.1.call-update) | async-done | bytes 33554448 | tf_op jit(solution)/shard_map/all_gather | solution.py:142
  908.2 16.1 %fusion.12 = f32[32,4096]{1,0:T(8,128)} fusion(bf16[4096,4096]{1,0:T(8,128)(2,1)} %all-gather.11.cloned.1.call-done, f32[32,4096]{1,0:T(8,128)} %reduce-scatter.2.cloned.1.call-done), kind=kOutput, calls=%fused_computation.24 | convolution fusion | flops 1073872896 | bytes 34603008 | tf_op jit(solution)/shard_map/dot_general | solution.py:140
  (80 shorter events, 61.4 us)
Async XLA Ops:
  7.2 85.2 %all-gather.7.cloned.1.call-start = ((), (), s32[]{:S(2)}) async-start(), calls=%async_computation.2 | async-start | bytes 8650752 | tf_op jit(solution)/shard_map/all_gather | solution.py:27
  7.9 163.4 %all-gather.9.cloned.1.call-start = ((), (), s32[]{:S(2)}) async-start(), calls=%async_computation.3 | async-start | bytes 8650752 | tf_op jit(solution)/shard_map/all_gather | solution.py:28
  8.6 241.6 %all-gather.5.cloned.1.call-start = ((), (), s32[]{:S(2)}) async-start(), calls=%async_computation.1 | async-start | bytes 8650752 | tf_op jit(solution)/shard_map/all_gather | solution.py:26
  9.4 699.6 %reduce-scatter.2.cloned.1.call-start = ((), (), s32[]{:S(2)}) async-start(), calls=%async_computation.4 | async-start | bytes 17301504 | tf_op jit(solution)/shard_map/reduce_scatter | solution.py:138
  250.2 11.0 %copy-start.7 = (s32[4]{0:T(128)S(1)}, s32[4]{0:T(128)}, u32[]{:S(2)}) copy-start(s32[4]{0:T(128)} %param.19) | copy-start | bytes 52
  299.1 1.6 copy-start.6
  300.7 8.5 copy-start.1
  300.7 8.5 copy-start.4
  309.1 3.8 copy-start
  310.3 1.3 copy-start.2
  311.6 1.3 copy-start.5
  365.6 1.6 copy-start.6
  367.2 8.5 copy-start.1
  367.2 8.5 copy-start.4
  375.7 3.8 copy-start
  376.8 1.3 copy-start.2
  378.1 1.3 copy-start.5
  395.2 1.6 copy-start.3
  395.2 513.0 %all-gather.11.cloned.1.call-start = ((), (), s32[]{:S(2)}) async-start(), calls=%async_computation.5 | async-start | bytes 34603008 | tf_op jit(solution)/shard_map/all_gather | solution.py:142
Sparse Core Ops, SparseCore 0:
  10.9 81.4 all-gather.6
  95.2 76.0 all-gather.8
  174.1 76.0 all-gather.4
  395.3 313.6 reduce-scatter.1
  711.7 196.3 all-gather.10
where the time goes:
time: 933 us; the launch traced here: 931 us
  waiting for transfers between devices  674 us (72%)
  local copies, waits for them, and re-layouts  86.1 us (9%)
  matrix products  83.1 us (9%)
  blocking collectives  45.4 us (5%)
  other arithmetic  20.8 us (2%)
  between operations  13.8 us (1%)
    reduce_scatter x1, waiting for transfers between devices, on_device(): lax.psum_scatter(query_terms, 'psg', scatter_dimension=0, tiled=True)  308 us
    all_gather x1, waiting for transfers between devices, on_device(): lax.all_gather(proj_weight, 'psg', axis=0, tiled=True)  199 us
    all_gather x1, waiting for transfers between devices, on_device(): lax.all_gather(attn_out, 'psg', axis=0, tiled=True)  78.9 us
    all_gather x1, waiting for transfers between devices, on_device(): lax.all_gather(queries, 'psg', axis=0, tiled=True)  56.1 us
    all_gather x1, blocking collectives, on_device(): all_lse = lax.all_gather(log_sum, 'psg', axis=1, tiled=True)  45.4 us
    all_gather x1, waiting for transfers between devices, on_device(): lax.all_gather(grad_out, 'psg', axis=0, tiled=True)  29.7 us
    dynamic_update_slice x4, local copies, waits for them, and re-layouts, visit(): lax.dynamic_update_slice_in_dim(grad_q, (asking_accumulator * inverse_roo...  20.5 us
    dot_general x2, matrix products, sub_visit(): jnp.einsum('dlyb,ilb->lydi', output_gradient_rows, value_block_rows, pref...  19.3 us
  transfers between devices with their start and end apart: 5, of which 5 were waited for; matrix products, arithmetic and copies ran while one was open for 4% of the time, Pallas kernels for 0%

commit v1 on v0

v1 whole, which is shorter than its diff:
```python
import functools

import jax
import jax.numpy as jnp
from jax import lax
from jax.experimental import pallas as pl
from jax.experimental.pallas import tpu as pltpu
from jax.sharding import PartitionSpec as P

ATTN_WIDTH = 128
GROUP = 4
PADDED_ASK_LEN = 256
TILE = 128
LOG2_E = 1.4426950408889634
SCALE = ATTN_WIDTH ** (-0.5)
NT = (((1,), (1,)), ((), ()))
NN = (((1,), (0,)), ((), ()))


def dot(a, b, dims=NN):
    return lax.dot_general(a, b, dims, preferred_element_type=jnp.float32)


def attention_kernel(
    blocks, tile_count, counts, tiles, kv_ref, q_ref, g_ref, ld_ref, dkv_ref, dq_ref, dk_acc, dv_acc, dq_acc
):
    block = pl.program_id(0)

    @pl.when(block == 0)
    def _():
        dq_acc[...] = jnp.zeros_like(dq_acc)

    dk_acc[...] = jnp.zeros_like(dk_acc)
    dv_acc[...] = jnp.zeros_like(dv_acc)
    key_rows_t = kv_ref[0, 0].T

    def visit(i, carry):
        tile = tiles[block, i]
        keys, values = kv_ref[0, 0], kv_ref[0, 1]
        dk, dv = None, None
        for part in range(2):
            rows = slice(part * 256, part * 256 + 256)
            q = q_ref[tile, rows, :]
            g = g_ref[tile, rows, :]
            lse = ld_ref[tile, 0:1, rows]
            delta = ld_ref[tile, 1:2, rows]
            prob = jnp.exp2(dot(keys, q, NT) * (SCALE * LOG2_E) - lse)
            dprob = dot(values, g, NT)
            dscore = (prob * (dprob - delta)).astype(jnp.bfloat16)
            v_term = dot(prob.astype(jnp.bfloat16), g)
            k_term = dot(dscore, q)
            dv = v_term if dv is None else dv + v_term
            dk = k_term if dk is None else dk + k_term
            dq_acc[tile, :, rows] += dot(key_rows_t, dscore)
        dk_acc[...] += dk
        dv_acc[...] += dv
        return carry

    lax.fori_loop(0, counts[block], visit, 0)
    dkv_ref[0, 0] = (dk_acc[...] * SCALE).astype(dkv_ref.dtype)
    dkv_ref[0, 1] = dv_acc[...].astype(dkv_ref.dtype)

    @pl.when(block == blocks - 1)
    def _():
        def put(tile, carry):
            for h in range(GROUP):
                cols = slice(h * ATTN_WIDTH, (h + 1) * ATTN_WIDTH)
                piece = dq_acc[tile, :, cols] * SCALE
                dq_ref[tile, :, cols] = piece.T.astype(dq_ref.dtype)
            return carry

        lax.fori_loop(0, tile_count, put, 0)


def attention(counts, tiles, kv, q, g, ld, out_dtype):
    blocks, _, span, width = kv.shape
    tile_count, lanes, _ = q.shape
    whole = lambda shape: pl.BlockSpec(shape, lambda b, *_: (0,) * len(shape))
    return pl.pallas_call(
        functools.partial(attention_kernel, blocks, tile_count),
        out_shape=(
            jax.ShapeDtypeStruct(kv.shape, out_dtype),
            jax.ShapeDtypeStruct((tile_count, TILE, lanes), jnp.bfloat16),
        ),
        grid_spec=pltpu.PrefetchScalarGridSpec(
            num_scalar_prefetch=2,
            grid=(blocks,),
            in_specs=[
                pl.BlockSpec((1, 2, span, width), lambda b, *_: (b, 0, 0, 0)),
                whole(q.shape),
                whole(g.shape),
                whole(ld.shape),
            ],
            out_specs=(
                pl.BlockSpec((1, 2, span, width), lambda b, *_: (b, 0, 0, 0)),
                whole((tile_count, TILE, lanes)),
            ),
            scratch_shapes=[
                pltpu.VMEM((span, width), jnp.float32),
                pltpu.VMEM((span, width), jnp.float32),
                pltpu.VMEM((tile_count, width, lanes), jnp.float32),
            ],
        ),
        compiler_params=pltpu.CompilerParams(vmem_limit_bytes=48 * 2**20),
        cost_estimate=pl.CostEstimate(
            flops=2 * blocks * span * width * lanes * tile_count * 5 // 2,
            bytes_accessed=16 * 2**20,
            transcendentals=blocks * span * lanes * tile_count // 2,
        ),
        name="attention",
    )(counts, tiles, kv, q, g, ld)


def on_device(queries, grad_out, attn_out, log_sum, keys, values, proj_weight, attend, qlen):
    row_count, columns = queries.shape
    head_count = log_sum.shape[0]
    slices = head_count // GROUP
    span = keys.shape[0]
    devices = lax.axis_size("psg")
    layers = devices // slices
    me = lax.axis_index("psg")
    lanes = GROUP * ATTN_WIDTH
    peers = [[z * slices + j for j in range(slices)] for z in range(layers)]
    per_tile = TILE // row_count
    tile_count = devices // per_tile

    kv = jnp.stack([keys, values]).reshape(2, span, slices, ATTN_WIDTH).transpose(2, 0, 1, 3)
    if slices > 1:
        kv = lax.all_to_all(kv, "psg", 0, 0, axis_index_groups=peers)

    qg = jnp.stack([queries, grad_out]).reshape(2, row_count, slices, GROUP, ATTN_WIDTH)
    qg = qg.transpose(2, 0, 3, 1, 4)
    qg = jnp.broadcast_to(qg[None], (layers,) + qg.shape).reshape((devices,) + qg.shape[1:])
    qg = lax.all_to_all(qg, "psg", 0, 0)
    qg = qg.reshape(tile_count, per_tile, 2, GROUP, row_count, ATTN_WIDTH)
    qg = qg.transpose(2, 0, 3, 1, 4, 5).reshape(2, tile_count, lanes, ATTN_WIDTH)

    products = grad_out.astype(jnp.float32) * attn_out.astype(jnp.float32)
    delta = jnp.sum(products.reshape(row_count, head_count, ATTN_WIDTH), axis=2).T
    ld = jnp.stack([log_sum * LOG2_E, delta])
    ld = ld.reshape(2, slices, GROUP, row_count).transpose(1, 0, 2, 3)
    ld = jnp.broadcast_to(ld[None], (layers,) + ld.shape).reshape((devices,) + ld.shape[1:])
    ld = lax.all_to_all(ld, "psg", 0, 0)
    ld = ld.reshape(tile_count, per_tile, 2, GROUP, row_count)
    ld = ld.transpose(0, 2, 3, 1, 4).reshape(tile_count, 2, lanes)

    block_ids = (me // slices) * slices + jnp.arange(slices, dtype=jnp.int32)
    named = jnp.any(attend[None] == block_ids[:, None, None], axis=2)
    tile_ids = jnp.arange(tile_count, dtype=jnp.int32)
    tile_start = tile_ids * TILE % PADDED_ASK_LEN
    tile_live = tile_start < jnp.repeat(qlen, PADDED_ASK_LEN // TILE)
    live = jnp.repeat(named, PADDED_ASK_LEN // TILE, axis=1) & tile_live[None]
    rank = jnp.cumsum(live.astype(jnp.int32), axis=1) - 1
    chosen = live[:, None, :] & (rank[:, None, :] == tile_ids[None, :, None])
    tiles = jnp.sum(jnp.where(chosen, tile_ids[None, None, :], 0), axis=2).astype(jnp.int32)
    counts = jnp.sum(live.astype(jnp.int32), axis=1)

    out_dtype = jnp.bfloat16 if slices > 1 else jnp.float32
    dkv, dq = attention(counts, tiles, kv, qg[0], qg[1], ld, out_dtype)

    dq = lax.all_to_all(dq.reshape(devices, row_count, lanes), "psg", 0, 0)
    dq = dq.reshape(layers, slices, row_count, lanes).astype(jnp.float32)
    grad_query = jnp.sum(dq, axis=0).transpose(1, 0, 2).reshape(row_count, columns)
    query_low = grad_query.astype(jnp.bfloat16)

    all_low = lax.all_gather(query_low, "psg", axis=0, tiled=True)
    hidden = dot(all_low, proj_weight, NT)
    out_columns = proj_weight.shape[0]
    hidden = lax.all_to_all(hidden.reshape(devices, row_count, out_columns), "psg", 0, 0)
    hidden = hidden.transpose(1, 0, 2).reshape(row_count, devices * out_columns)
    grad_hidden = lax.psum(hidden, "qry")

    if slices > 1:
        dkv = lax.all_to_all(dkv, "psg", 0, 0, axis_index_groups=peers)
    dkv = dkv.astype(jnp.float32).transpose(1, 2, 0, 3).reshape(2, span, slices * ATTN_WIDTH)
    return (grad_query, dkv[0], dkv[1], grad_hidden)


def solution(mesh):
    in_specs = (
        P("psg", "qry"),
        P("psg", "qry"),
        P("psg", "qry"),
        P("qry", "psg"),
        P("psg", "qry"),
        P("psg", "qry"),
        P("psg", "qry"),
        P(),
        P(),
    )
    out_specs = (P("psg", "qry"), P("psg", "qry"), P("psg", "qry"), P("psg", None))
    return jax.shard_map(
        on_device, mesh=mesh, in_specs=in_specs, out_specs=out_specs, check_vma=False
    )
```

time: 933 us -> 295 us (0.32)
  waiting for transfers between devices: 674 us -> 151 us
  matrix products: 83.1 us -> 6.51 us
  local copies, waits for them, and re-layouts: 86.1 us -> 26.8 us
  Pallas kernels: 0 us -> 41.3 us
  starting transfers between devices: 0.41 us -> 21.4 us
  blocking collectives: 45.4 us -> 27.9 us
  other arithmetic: 20.8 us -> 8.32 us
    reduce_scatter x1 -> x0, waiting for transfers between devices: 308 us -> none  [on_device(): lax.psum_scatter(query_terms, 'psg', scatter_dimension=0, tiled=True)]
    all_gather x4 -> x1, waiting for transfers between devices: 364 us -> 79 us  [on_device(): all_low = lax.all_gather(query_low, 'psg', axis=0, tiled=True)]
    dot_general x11 -> x1, matrix products: 83.1 us -> 6.51 us  [dot(): return lax.dot_general(a, b, dims, preferred_element_type=jnp.float32)]
    all_to_all x0 -> x5, waiting for transfers between devices: none -> 71.5 us  [the longest x1 36.8 us: on_device(): qg = lax.all_to_all(qg, 'psg', 0, 0)]
    all_gather x1 -> x0, blocking collectives: 45.4 us -> none  [on_device(): all_lse = lax.all_gather(log_sum, 'psg', axis=1, tiled=True)]
    pallas_call x0 -> x1, Pallas kernels: none -> 41.3 us  [attention(): pl.pallas_call(functools.partial(attention_kernel, blocks, tile_count), o...]
    dynamic_slice x16 -> x0, local copies, waits for them, and re-layouts: 29.7 us -> none  [the longest x4 14.5 us: visit(): lax.dynamic_slice_in_dim(all_grads, row_start, PADDED_ASK_LEN, 0)]
    all_to_all x0 -> x1, blocking collectives: none -> 27.9 us  [on_device(): dq = lax.all_to_all(dq.reshape(devices, row_count, lanes), 'psg', 0, 0)]
  transfers between devices with their start and end apart: 5 -> 6, of which waited for: 5 -> 5; matrix products, arithmetic and copies ran while one was open for 4% -> 11% of each run, Pallas kernels for 0% -> 0%
where the time goes in v1:
time: 295 us; the launch traced here: 297 us
  waiting for transfers between devices  151 us (51%)
  Pallas kernels  41.3 us (14%)
  blocking collectives  27.9 us (9%)
  local copies, waits for them, and re-layouts  26.8 us (9%)
  starting transfers between devices  21.4 us (7%)
  between operations  14.3 us (5%)
  other arithmetic  8.32 us (3%)
  matrix products  6.51 us (2%)
    all_gather x1, waiting for transfers between devices, on_device(): all_low = lax.all_gather(query_low, 'psg', axis=0, tiled=True)  79 us
    pallas_call x1, Pallas kernels, attention(): pl.pallas_call(functools.partial(attention_kernel, blocks, tile_count), o...  41.3 us
    all_to_all x1, waiting for transfers between devices, on_device(): qg = lax.all_to_all(qg, 'psg', 0, 0)  36.8 us
    all_to_all x1, blocking collectives, on_device(): dq = lax.all_to_all(dq.reshape(devices, row_count, lanes), 'psg', 0, 0)  27.9 us
    all_to_all x1, waiting for transfers between devices, on_device(): kv = lax.all_to_all(kv, 'psg', 0, 0, axis_index_groups=peers)  23.1 us
    unnamed x19, local copies, waits for them, and re-layouts  9.96 us
    all_to_all x1, starting transfers between devices, on_device(): ld = lax.all_to_all(ld, 'psg', 0, 0)  7.3 us
    dot_general x1, matrix products, dot(): return lax.dot_general(a, b, dims, preferred_element_type=jnp.float32)  6.51 us
  transfers between devices with their start and end apart: 6, of which 5 were waited for; matrix products, arithmetic and copies ran while one was open for 11% of the time, Pallas kernels for 0%

profile of v1, /device:TPU:0, one launch (start us, length us, event | category | flops | bytes accessed | tf_op | source)
XLA Modules:
  0.0 297.2 jit_solution(9637749574760933633)
XLA Ops:
  10.3 7.3 %all-to-all-start.2 = ((f32[32,1,256]{2,1,0:T(1,128)}), f32[32,1,256]{2,1,0:T(1,128)S(1)}, u32[]{:S(2)}, u32[]{:S(2)}) async-start(f32[32,1,256]{2,1,0:T(1,128)} %reshape.155), calls=%async_computation.2 | async-start | bytes 65536 | tf_op jit(solution)/shard_map/all_to_all | solution.py:143
  18.6 6.3 %all-to-all-done.2 = f32[32,1,256]{2,1,0:T(1,128)S(1)} async-done(((f32[32,1,256]{2,1,0:T(1,128)}), f32[32,1,256]{2,1,0:T(1,128)S(1)}, u32[]{:S(2)}, u32[]{:S(2)}) %all-to-all-start.2) | async-done | bytes 32800 | tf_op jit(solution)/shard_map/all_to_all | solution.py:143
  24.9 1.8 broadcast_in_dim.20
  26.7 2.7 all-to-all-start.1
  29.5 2.3 copy.73
  31.7 2.3 copy.75
  34.0 2.3 copy.74
  36.3 2.3 copy.76
  38.5 3.1 %maximum_bitcast_fusion = bf16[8,2,512,128]{3,2,1,0:T(8,128)(2,1)} fusion(bf16[1,512,8,128]{3,1,0,2:T(8,128)(2,1)} %copy.76, bf16[1,512,8,128]{3,1,0,2:T(8,128)(2,1)} %copy.75), kind=kLoop, calls=%fused_computation.1 | loop fusion | flops 1048576 | bytes 4194304 | tf_op jit(solution)/shard_map/transpose | solution.py:127
  41.6 36.8 %all-to-all-done.1 = bf16[32,2,4,32,128]{4,3,2,1,0:T(8,128)(2,1)S(1)} async-done(((bf16[32,2,4,32,128]{4,3,2,1,0:T(8,128)(2,1)}), bf16[32,2,4,32,128]{4,3,2,1,0:T(8,128)(2,1)S(1)}, u32[]{:S(2)}, u32[]{:S(2)}) %all-to-all-start.1) | async-done | bytes 2097184 | tf_op jit(solution)/shard_map/all_to_all | solution.py:134
  78.4 4.3 %all-to-all-start = ((bf16[8,2,512,128]{3,2,1,0:T(8,128)(2,1)}), bf16[8,2,512,128]{3,2,1,0:T(8,128)(2,1)}, u32[]{:S(2)}, u32[]{:S(2)}) async-start(bf16[8,2,512,128]{3,2,1,0:T(8,128)(2,1)} %maximum_bitcast_fusion), calls=%async_computation | async-start | bytes 4194304 | tf_op jit(solution)/shard_map/all_to_all | solution.py:129
  86.3 23.1 %all-to-all-done.kv_ref = bf16[8,2,512,128]{3,2,1,0:T(8,128)(2,1)} async-done(((bf16[8,2,512,128]{3,2,1,0:T(8,128)(2,1)}), bf16[8,2,512,128]{3,2,1,0:T(8,128)(2,1)}, u32[]{:S(2)}, u32[]{:S(2)}) %all-to-all-start) | async-done | bytes 2097184 | tf_op jit(solution)/shard_map/all_to_all | solution.py:129
  109.4 41.3 %attention.1 = (bf16[8,2,512,128]{3,2,1,0:T(8,128)(2,1)}, bf16[8,128,512]{2,1,0:T(8,128)(2,1)S(1)}) custom-call(s32[8]{0:T(128)S(1)} %fusion.1.counts, s32[8,8]{1,0:T(8,128)S(1)} %select_reduce_fusion.tiles, bf16[8,2,512,128]{3,2,1,0:T(8,128)(2,1)} %all-to-all-done.kv_ref, bf16[8,512,128]{2,1,0:T(8,128)(2,1)S(1)} %bitcast.46, ...), custom_call_target="tpu_custom_call" | custom-call | flops 10737418240 | bytes 16777216 | tf_op jit(solution)/shard_map/attention/pallas_call | solution.py:79
  150.7 27.9 %all_to_all.30 = bf16[32,32,512]{2,1,0:T(8,128)(2,1)S(1)} all-to-all(bf16[32,32,512]{2,1,0:T(8,128)(2,1)S(1)} %bitcast.47), channel_id=1, replica_groups=mesh['psg'=32,'qry'=1] {'psg'}, dimensions={0} | all-to-all | bytes 2097152 | tf_op jit(solution)/shard_map/all_to_all | solution.py:161
  180.4 3.7 %all-to-all-start.4 = ((bf16[8,2,512,128]{3,2,1,0:T(8,128)(2,1)}), bf16[8,2,512,128]{3,2,1,0:T(8,128)(2,1)S(1)}, u32[]{:S(2)}, u32[]{:S(2)}) async-start(bf16[8,2,512,128]{3,2,1,0:T(8,128)(2,1)} %get-tuple-element.7), calls=%async_computation.4 | async-start | bytes 4194304 | tf_op jit(solution)/shard_map/all_to_all | solution.py:174
  184.1 79.0 %all-gather.2.cloned.1.call-done = bf16[1024,4096]{1,0:T(8,128)(2,1)} async-done(((bf16[32,4096]{1,0:T(8,128)(2,1)}), bf16[1024,4096]{1,0:T(8,128)(2,1)}) %all-gather.2.cloned.1.call-update) | async-done | bytes 8388624 | tf_op jit(solution)/shard_map/all_gather | solution.py:166
  263.1 6.5 %fusion.9 = f32[1024,128]{1,0:T(8,128)} fusion(bf16[1024,4096]{1,0:T(8,128)(2,1)} %all-gather.2.cloned.1.call-done, bf16[128,4096]{1,0:T(8,128)(2,1)S(1)} %copy-done), kind=kOutput, calls=%fused_computation.30 | convolution fusion | flops 1073741824 | bytes 9961472 | tf_op jit(solution)/shard_map/dot_general | solution.py:21
  269.7 3.3 %all-to-all-start.5 = ((f32[32,32,128]{2,1,0:T(8,128)}), f32[32,32,128]{2,1,0:T(8,128)}, u32[]{:S(2)}, u32[]{:S(2)}) async-start(f32[32,32,128]{2,1,0:T(8,128)} %bitcast.59), calls=%async_computation.5 | async-start | bytes 1048576 | tf_op jit(solution)/shard_map/all_to_all | solution.py:169
  273.4 2.3 fusion.7
  275.7 1.9 copy.86
  277.7 1.8 copy.89
  279.5 1.9 copy.85
  283.2 5.3 %all-to-all-done.5 = f32[32,32,128]{2,1,0:T(8,128)} async-done(((f32[32,32,128]{2,1,0:T(8,128)}), f32[32,32,128]{2,1,0:T(8,128)}, u32[]{:S(2)}, u32[]{:S(2)}) %all-to-all-start.5) | async-done | bytes 524320 | tf_op jit(solution)/shard_map/all_to_all | solution.py:169
  288.5 1.9 copy_bitcast_fusion
  (57 shorter events, 11.4 us)
Async XLA Ops:
  7.2 256.0 %copy-start = (bf16[128,4096]{1,0:T(8,128)(2,1)S(1)}, bf16[128,4096]{1,0:T(8,128)(2,1)}, u32[]{:S(2)}) copy-start(bf16[128,4096]{1,0:T(8,128)(2,1)} %param.15) | copy-start | bytes 3145732
  7.2 10.5 %copy-start.2 = (bf16[32,4096]{1,0:T(8,128)(2,1)S(1)}, bf16[32,4096]{1,0:T(8,128)(2,1)}, u32[]{:S(2)}) copy-start(bf16[32,4096]{1,0:T(8,128)(2,1)} %param.10) | copy-start | bytes 786436
  7.2 10.6 %copy-start.3 = (bf16[32,4096]{1,0:T(8,128)(2,1)S(1)}, bf16[32,4096]{1,0:T(8,128)(2,1)}, u32[]{:S(2)}) copy-start(bf16[32,4096]{1,0:T(8,128)(2,1)} %param.9) | copy-start | bytes 786436
  10.3 14.6 %all-to-all-start.2 = ((f32[32,1,256]{2,1,0:T(1,128)}), f32[32,1,256]{2,1,0:T(1,128)S(1)}, u32[]{:S(2)}, u32[]{:S(2)}) async-start(f32[32,1,256]{2,1,0:T(1,128)} %reshape.155), calls=%async_computation.2 | async-start | bytes 65536 | tf_op jit(solution)/shard_map/all_to_all | solution.py:143
  26.7 51.7 %all-to-all-start.1 = ((bf16[32,2,4,32,128]{4,3,2,1,0:T(8,128)(2,1)}), bf16[32,2,4,32,128]{4,3,2,1,0:T(8,128)(2,1)S(1)}, u32[]{:S(2)}, u32[]{:S(2)}) async-start(bf16[32,2,4,32,128]{4,3,2,1,0:T(8,128)(2,1)} %bitcast.4), calls=%async_computation.1 | async-start | bytes 4194304 | tf_op jit(solution)/shard_map/all_to_all | solution.py:134
  41.6 41.2 %copy-start.4 = (s32[4,16]{1,0:T(4,128)S(1)}, s32[4,16]{1,0:T(4,128)}, u32[]{:S(2)}) copy-start(s32[4,16]{1,0:T(4,128)} %param.16) | copy-start | bytes 772
  41.6 41.5 %copy-start.5 = (s32[4]{0:T(128)S(1)}, s32[4]{0:T(128)}, u32[]{:S(2)}) copy-start(s32[4]{0:T(128)} %param.17) | copy-start | bytes 52
  78.4 31.0 %all-to-all-start = ((bf16[8,2,512,128]{3,2,1,0:T(8,128)(2,1)}), bf16[8,2,512,128]{3,2,1,0:T(8,128)(2,1)}, u32[]{:S(2)}, u32[]{:S(2)}) async-start(bf16[8,2,512,128]{3,2,1,0:T(8,128)(2,1)} %maximum_bitcast_fusion), calls=%async_computation | async-start | bytes 4194304 | tf_op jit(solution)/shard_map/all_to_all | solution.py:129
  82.7 180.4 %all-gather.2.cloned.1.call-start = ((), (), s32[]{:S(2)}) async-start(), calls=%async_computation.6 | async-start | bytes 8650752 | tf_op jit(solution)/shard_map/all_gather | solution.py:166
  178.9 0.8 copy-start.1
  180.4 89.2 %all-to-all-start.4 = ((bf16[8,2,512,128]{3,2,1,0:T(8,128)(2,1)}), bf16[8,2,512,128]{3,2,1,0:T(8,128)(2,1)S(1)}, u32[]{:S(2)}, u32[]{:S(2)}) async-start(bf16[8,2,512,128]{3,2,1,0:T(8,128)(2,1)} %get-tuple-element.7), calls=%async_computation.4 | async-start | bytes 4194304 | tf_op jit(solution)/shard_map/all_to_all | solution.py:174
  269.7 18.9 %all-to-all-start.5 = ((f32[32,32,128]{2,1,0:T(8,128)}), f32[32,32,128]{2,1,0:T(8,128)}, u32[]{:S(2)}, u32[]{:S(2)}) async-start(f32[32,32,128]{2,1,0:T(8,128)} %bitcast.59), calls=%async_computation.5 | async-start | bytes 1048576 | tf_op jit(solution)/shard_map/all_to_all | solution.py:169
Sparse Core Ops, SparseCore 0:
  180.5 82.5 all-gather.1

commit v2 on v1

v2 whole, which is shorter than its diff:
```python
import functools

import jax
import jax.numpy as jnp
from jax import lax
from jax.experimental import pallas as pl
from jax.experimental.pallas import tpu as pltpu
from jax.sharding import PartitionSpec as P

ATTN_WIDTH = 128
GROUP = 4
PADDED_ASK_LEN = 256
TILE = 128
LOG2_E = 1.4426950408889634
SCALE = ATTN_WIDTH ** (-0.5)
NT = (((1,), (1,)), ((), ()))
NN = (((1,), (0,)), ((), ()))


def dot(a, b, dims=NN):
    return lax.dot_general(a, b, dims, preferred_element_type=jnp.float32)


def attention_kernel(
    blocks, tile_count, per_tile, counts, tiles, kv_ref, qg_ref, ld_ref, dkv_ref, dq_ref, dk_acc, dv_acc, dq_acc
):
    block = pl.program_id(0)
    per_part = per_tile // 2
    wide = GROUP * TILE // per_tile

    @pl.when(block == 0)
    def _():
        dq_acc[...] = jnp.zeros_like(dq_acc)

    dk_acc[...] = jnp.zeros_like(dk_acc)
    dv_acc[...] = jnp.zeros_like(dv_acc)
    key_rows_t = kv_ref[0, 0].T

    def visit(i, carry):
        tile = tiles[block, i]
        keys, values = kv_ref[0, 0], kv_ref[0, 1]
        dk, dv = None, None
        for part in range(2):
            rows = slice(part * 256, part * 256 + 256)
            first = tile * per_tile + part * per_part
            q = qg_ref[pl.ds(first, per_part), 0].reshape(256, ATTN_WIDTH)
            g = qg_ref[pl.ds(first, per_part), 1].reshape(256, ATTN_WIDTH)
            ld = jnp.concatenate([ld_ref[first + k] for k in range(per_part)], axis=1)
            lse, delta = ld[0:1], ld[1:2]
            prob = jnp.exp2(dot(keys, q, NT) * (SCALE * LOG2_E) - lse)
            dprob = dot(values, g, NT)
            dscore = (prob * (dprob - delta)).astype(jnp.bfloat16)
            v_term = dot(prob.astype(jnp.bfloat16), g)
            k_term = dot(dscore, q)
            dv = v_term if dv is None else dv + v_term
            dk = k_term if dk is None else dk + k_term
            dq_acc[tile, :, rows] += dot(key_rows_t, dscore)
        dk_acc[...] += dk
        dv_acc[...] += dv
        return carry

    lax.fori_loop(0, counts[block], visit, 0)
    dkv_ref[0, 0] = (dk_acc[...] * SCALE).astype(dkv_ref.dtype)
    dkv_ref[0, 1] = dv_acc[...].astype(dkv_ref.dtype)

    @pl.when(block == blocks - 1)
    def _():
        def put(tile, carry):
            for k in range(per_tile):
                piece = dq_acc[tile, :, k * wide : (k + 1) * wide] * SCALE
                dq_ref[tile * per_tile + k] = piece.T.astype(dq_ref.dtype)
            return carry

        lax.fori_loop(0, tile_count, put, 0)


def attention(counts, tiles, kv, qg, ld, out_dtype):
    blocks, _, span, width = kv.shape
    sources, _, wide, _ = qg.shape
    lanes = GROUP * TILE
    per_tile = lanes // wide
    tile_count = sources // per_tile
    whole = lambda shape: pl.BlockSpec(shape, lambda b, *_: (0,) * len(shape))
    return pl.pallas_call(
        functools.partial(attention_kernel, blocks, tile_count, per_tile),
        out_shape=(
            jax.ShapeDtypeStruct(kv.shape, out_dtype),
            jax.ShapeDtypeStruct((sources, wide, width), jnp.bfloat16),
        ),
        grid_spec=pltpu.PrefetchScalarGridSpec(
            num_scalar_prefetch=2,
            grid=(blocks,),
            in_specs=[
                pl.BlockSpec((1, 2, span, width), lambda b, *_: (b, 0, 0, 0)),
                whole(qg.shape),
                whole(ld.shape),
            ],
            out_specs=(
                pl.BlockSpec((1, 2, span, width), lambda b, *_: (b, 0, 0, 0)),
                whole((sources, wide, width)),
            ),
            scratch_shapes=[
                pltpu.VMEM((span, width), jnp.float32),
                pltpu.VMEM((span, width), jnp.float32),
                pltpu.VMEM((tile_count, width, lanes), jnp.float32),
            ],
        ),
        compiler_params=pltpu.CompilerParams(vmem_limit_bytes=48 * 2**20),
        cost_estimate=pl.CostEstimate(
            flops=2 * blocks * span * width * lanes * tile_count * 5 // 2,
            bytes_accessed=16 * 2**20,
            transcendentals=blocks * span * lanes * tile_count // 2,
        ),
        name="attention",
    )(counts, tiles, kv, qg, ld)


def routes(kind, devices, slices, me):
    layers = devices // slices
    j, z = lax.rem(me, slices), me // slices
    base = me - j
    if kind in ("all", "cast"):

        def step(r):
            target = lax.rem(me + r, devices)
            return target, (target if kind == "all" else lax.rem(target, slices)), me

        return devices, step
    if kind == "layer":

        def step(r):
            other = lax.rem(j + r, slices)
            return base + other, other, j

        return slices, step
    if kind == "z":

        def step(r):
            other = lax.rem(z + r, layers)
            return other * slices + j, other, z

        return layers, step
    quads = slices // 2

    def step(r):
        other = lax.rem(j // 2 + r, quads)
        return base + 2 * other + lax.rem(j, 2), other, j // 2

    return quads, step


def repeat(first, count, body):
    if count - first <= 8:
        for r in range(first, count):
            body(r)
    else:
        lax.fori_loop(first, count, lambda r, c: (body(r), c)[1], 0)


def exchange_kernel(kinds, devices, slices, gathered, *refs):
    n = len(kinds)
    total = n + gathered
    sources, outs = refs[:total], refs[total : 2 * total]
    sems = refs[2 * total :]
    me = lax.axis_index("psg")
    barrier = pltpu.get_barrier_semaphore()
    if "all" in kinds or "cast" in kinds:
        greeted = ("all",)
    else:
        greeted = ("z", "layer")
    count = 0
    for kind in greeted:
        size, step = routes(kind, devices, slices, me)
        count += size - 1

        def greet(r, step=step):
            pl.semaphore_signal(barrier, inc=1, device_id={"psg": step(r)[0]}, device_id_type=pl.DeviceIdType.MESH)

        repeat(1, size, greet)
    pl.semaphore_wait(barrier, count)

    def remote(src, dst, send, recv, target):
        return pltpu.make_async_remote_copy(
            src_ref=src,
            dst_ref=dst,
            send_sem=send,
            recv_sem=recv,
            device_id={"psg": target},
            device_id_type=pl.DeviceIdType.MESH,
        )

    if gathered:
        j, z = lax.rem(me, slices), me // slices
        parity = lax.rem(j, 2)
        partner = me + 1 - 2 * parity
        layers = devices // slices
        mine, pair = sources[n], outs[n]
        send, recv, pair_send, pair_recv, own = sems[3 * n :]
        along = []
        for r in range(1, layers):
            target = lax.rem(z + r, layers) * slices + j
            along.append(remote(mine, pair.at[parity, z], send.at[r], recv.at[r], target))
            along[-1].start()
        across = [remote(mine, pair.at[parity, z], pair_send.at[0], pair_recv.at[0], partner)]
        across[0].start()
        kept = pltpu.make_async_copy(mine, pair.at[parity, z], own)
        kept.start()

    moves, stays = [], []
    for i, kind in enumerate(kinds):
        size, step = routes(kind, devices, slices, me)

        def copy(r, i=i, step=step):
            target, chunk, slot = step(r)
            return remote(
                sources[i].at[chunk], outs[i].at[slot], sems[3 * i].at[r], sems[3 * i + 1].at[r], target
            )

        moves.append((size, copy))
        chunk, slot = step(0)[1:]
        stays.append(pltpu.make_async_copy(sources[i].at[chunk], outs[i].at[slot], sems[3 * i + 2]))
    for size, copy in moves:
        repeat(1, size, lambda r, copy=copy: copy(r).start())
    for stay in stays:
        stay.start()

    if gathered:
        for r in range(1, layers):
            along[r - 1].wait_recv()
            landed = pair.at[parity, lax.rem(z - r + layers, layers)]
            across.append(remote(landed, landed, pair_send.at[r], pair_recv.at[r], partner))
            across[-1].start()
        for copy in along:
            copy.wait_send()
        for copy in across:
            copy.wait()
        kept.wait()
    for stay in stays:
        stay.wait()
    for size, copy in moves:
        repeat(1, size, lambda r, copy=copy: copy(r).wait())


def exchange(name, number, devices, slices, parts, gather=None):
    kinds = tuple(kind for kind, _ in parts)
    arrays = [array for _, array in parts]
    layers = devices // slices
    sizes = {"all": devices, "cast": devices, "layer": slices, "z": layers, "parity": slices // 2}
    shapes = [
        jax.ShapeDtypeStruct((sizes[kind],) + array.shape[1:], array.dtype) for kind, array in parts
    ]
    scratch = []
    for kind in kinds:
        scratch += [pltpu.SemaphoreType.DMA((sizes[kind],))] * 2 + [pltpu.SemaphoreType.DMA]
    if gather is not None:
        arrays.append(gather)
        shapes.append(jax.ShapeDtypeStruct((2, layers) + gather.shape, gather.dtype))
        scratch += [pltpu.SemaphoreType.DMA((layers,))] * 4 + [pltpu.SemaphoreType.DMA]
    anywhere = pl.BlockSpec(memory_space=pl.ANY)
    return pl.pallas_call(
        functools.partial(exchange_kernel, kinds, devices, slices, int(gather is not None)),
        out_shape=tuple(shapes),
        in_specs=[anywhere] * len(arrays),
        out_specs=tuple([anywhere] * len(shapes)),
        scratch_shapes=scratch,
        compiler_params=pltpu.CompilerParams(collective_id=number, has_side_effects=True),
        cost_estimate=pl.CostEstimate(flops=0, bytes_accessed=60 * 2**20, transcendentals=0),
        name=name,
    )(*arrays)


def on_device(queries, grad_out, attn_out, log_sum, keys, values, proj_weight, attend, qlen):
    row_count, columns = queries.shape
    head_count = log_sum.shape[0]
    slices = head_count // GROUP
    span = keys.shape[0]
    devices = lax.axis_size("psg")
    layers = devices // slices
    me = lax.axis_index("psg")
    lanes = GROUP * ATTN_WIDTH
    wide = GROUP * row_count
    tile_count = devices * row_count // TILE
    run = functools.partial(exchange, devices=devices, slices=slices)

    kv = jnp.stack([keys, values]).reshape(2, span, slices, ATTN_WIDTH).transpose(2, 0, 1, 3)
    qg = jnp.stack([queries, grad_out]).reshape(2, row_count, slices, GROUP, ATTN_WIDTH)
    qg = qg.transpose(2, 0, 3, 1, 4).reshape(slices, 2, wide, ATTN_WIDTH)
    products = grad_out.astype(jnp.float32) * attn_out.astype(jnp.float32)
    delta = jnp.sum(products.reshape(row_count, head_count, ATTN_WIDTH), axis=2).T
    ld = jnp.stack([log_sum * LOG2_E, delta])
    ld = ld.reshape(2, slices, wide).transpose(1, 0, 2)
    if slices > 1:
        qg, ld, kv = run("exchange_in", 0, parts=[("cast", qg), ("cast", ld), ("layer", kv)])
    else:
        qg, ld = run("exchange_in", 0, parts=[("cast", qg), ("cast", ld)])

    block_ids = (me // slices) * slices + jnp.arange(slices, dtype=jnp.int32)
    named = jnp.any(attend[None] == block_ids[:, None, None], axis=2)
    tile_ids = jnp.arange(tile_count, dtype=jnp.int32)
    tile_start = tile_ids * TILE % PADDED_ASK_LEN
    tile_live = tile_start < jnp.repeat(qlen, PADDED_ASK_LEN // TILE)
    live = jnp.repeat(named, PADDED_ASK_LEN // TILE, axis=1) & tile_live[None]
    rank = jnp.cumsum(live.astype(jnp.int32), axis=1) - 1
    chosen = live[:, None, :] & (rank[:, None, :] == tile_ids[None, :, None])
    tiles = jnp.sum(jnp.where(chosen, tile_ids[None, None, :], 0), axis=2).astype(jnp.int32)
    counts = jnp.sum(live.astype(jnp.int32), axis=1)

    out_dtype = jnp.bfloat16 if slices > 1 else jnp.float32
    dkv, dq = attention(counts, tiles, kv, qg, ld, out_dtype)

    dq = dq.reshape(layers, slices, wide, ATTN_WIDTH)
    if slices > 1:
        dq, dkv = run("exchange_terms", 1, parts=[("z", dq), ("layer", dkv)])
    else:
        (dq,) = run("exchange_terms", 1, parts=[("all", dq)])
    summed = jnp.sum(dq.astype(jnp.float32), axis=0)
    low = summed.astype(jnp.bfloat16).reshape(slices, GROUP, row_count, ATTN_WIDTH)
    low = low.transpose(0, 2, 1, 3).reshape(slices * row_count, lanes)

    out_columns = proj_weight.shape[0]
    if slices > 1:
        weight = proj_weight.reshape(out_columns, slices // 2, 2 * lanes).transpose(1, 0, 2)
        summed, weight, low = run(
            "exchange_rows", 2, parts=[("layer", summed), ("parity", weight)], gather=low
        )
        low = low.reshape(2, devices * row_count, lanes)
        weight = weight.reshape(slices // 2 * out_columns, 2 * lanes)
        hidden = dot(low[0], weight[:, :lanes], NT) + dot(low[1], weight[:, lanes:], NT)
        hidden = hidden.astype(jnp.bfloat16).reshape(devices, row_count, slices // 2 * out_columns)
        (hidden,) = run("exchange_hidden", 3, parts=[("all", hidden)])
        hidden = hidden.reshape(layers, slices // 2, 2, row_count, slices // 2, out_columns)
        hidden = jnp.sum(hidden.astype(jnp.float32), axis=1)
        hidden = hidden.transpose(2, 0, 3, 1, 4).reshape(row_count, devices * out_columns)
    else:
        all_low = lax.all_gather(low, "psg", axis=0, tiled=True)
        hidden = dot(all_low, proj_weight, NT)
        hidden = lax.all_to_all(hidden.reshape(devices, row_count, out_columns), "psg", 0, 0)
        hidden = hidden.transpose(1, 0, 2).reshape(row_count, devices * out_columns)
    grad_hidden = lax.psum(hidden, "qry")

    grad_query = summed.reshape(slices, GROUP, row_count, ATTN_WIDTH)
    grad_query = grad_query.transpose(2, 0, 1, 3).reshape(row_count, columns)
    dkv = dkv.astype(jnp.float32).transpose(1, 2, 0, 3).reshape(2, span, slices * ATTN_WIDTH)
    return (grad_query, dkv[0], dkv[1], grad_hidden)


def solution(mesh):
    in_specs = (
        P("psg", "qry"),
        P("psg", "qry"),
        P("psg", "qry"),
        P("qry", "psg"),
        P("psg", "qry"),
        P("psg", "qry"),
        P("psg", "qry"),
        P(),
        P(),
    )
    out_specs = (P("psg", "qry"), P("psg", "qry"), P("psg", "qry"), P("psg", None))
    return jax.shard_map(
        on_device, mesh=mesh, in_specs=in_specs, out_specs=out_specs, check_vma=False
    )
```

time: 295 us -> 221 us (0.75)
  the two profiles are of different devices: /device:TPU:0 before, /device:TPU:15 now
where the time goes in v2:
time: 221 us; the launch traced here: 223 us
  Pallas kernels  181 us (82%)
  local copies, waits for them, and re-layouts  30.6 us (14%)
  other arithmetic  8.59 us (4%)
  matrix products  2.45 us (1%)
    pallas_call x4, Pallas kernels, exchange(): pl.pallas_call(functools.partial(exchange_kernel, kinds, devices, slices,...  145 us
    pallas_call x1, Pallas kernels, attention(): pl.pallas_call(functools.partial(attention_kernel, blocks, tile_count, pe...  35.9 us
    unnamed x33, local copies, waits for them, and re-layouts  11.9 us
    slice x3, local copies, waits for them, and re-layouts, on_device(): return (grad_query, dkv[0], dkv[1], grad_hidden)  6.15 us

profile of v2, /device:TPU:15, one launch (start us, length us, event | category | flops | bytes accessed | tf_op | source)
XLA Modules:
  0.0 223.3 jit_solution(14014236579841016574)
XLA Ops:
  4.6 1.1 stack.27
  5.8 1.1 stack.28
  11.5 1.5 maximum_bitcast_fusion.refs_2_
  13.7 1.3 copy.80
  15.0 58.5 %exchange_in.1 = (bf16[32,2,128,128]{3,2,1,0:T(8,128)(2,1)}, f32[32,2,128]{2,1,0:T(2,128)}, bf16[8,2,512,128]{3,2,1,0:T(8,128)(2,1)}) custom-call(bf16[8,2,128,128]{3,2,1,0:T(8,128)(2,1)} %bitcast.49, f32[8,2,128]{2,1,0:T(2,128)} %maximum_bitcast_fusion.1.refs_1_, bf16[8,2,512,128]{3,2,1,0:T(8,128)(2,1)} %maximum_bitcast_fusion.refs_2_), custom_call_target="tpu_custom_call" | custom-call | bytes 62914560 | tf_op jit(solution)/shard_map/exchange_in/pallas_call | solution.py:260
  73.6 1.6 copy-done.2
  75.9 35.9 %attention.1 = (bf16[8,2,512,128]{3,2,1,0:T(8,128)(2,1)S(1)}, bf16[32,128,128]{2,1,0:T(8,128)(2,1)S(1)}) custom-call(s32[8]{0:T(128)S(1)} %fusion.4.counts, s32[8,8]{1,0:T(8,128)S(1)} %select_reduce_fusion.tiles, bf16[8,2,512,128]{3,2,1,0:T(8,128)(2,1)S(1)} %copy-done.2, bf16[32,2,128,128]{3,2,1,0:T(8,128)(2,1)} %get-tuple-element.15.qg_ref, ...), custom_call_target="tpu_custom_call" | custom-call | flops 10737418240 | bytes 16777216 | tf_op jit(solution)/shard_map/attention/pallas_call | solution.py:84
  111.9 1.3 copy-done
  113.2 1.0 copy-done.1
  114.2 28.3 %exchange_terms.1 = (bf16[4,8,128,128]{3,2,1,0:T(8,128)(2,1)}, bf16[8,2,512,128]{3,2,1,0:T(8,128)(2,1)}) custom-call(bf16[4,8,128,128]{3,2,1,0:T(8,128)(2,1)} %bitcast.39, bf16[8,2,512,128]{3,2,1,0:T(8,128)(2,1)} %copy-done), custom_call_target="tpu_custom_call" | custom-call | bytes 62914560 | tf_op jit(solution)/shard_map/exchange_terms/pallas_call | solution.py:260
  142.5 1.4 convert_reduce_fusion.refs_0_
  144.9 28.7 %exchange_rows.1 = (f32[8,128,128]{2,1,0:T(8,128)}, bf16[4,128,1024]{2,1,0:T(8,128)(2,1)}, bf16[2,4,256,512]{3,2,1,0:T(8,128)(2,1)}) custom-call(f32[8,128,128]{2,1,0:T(8,128)} %copy-done.4, bf16[4,128,1024]{2,1,0:T(8,128)(2,1)} %bitcast.42, bf16[256,512]{1,0:T(8,128)(2,1)} %bitcast.54), custom_call_target="tpu_custom_call" | custom-call | bytes 62914560 | tf_op jit(solution)/shard_map/exchange_rows/pallas_call | solution.py:260
  173.6 1.5 copy.82
  175.1 1.0 reshape.151
  176.3 1.0 copy-done.7
  178.1 1.7 add_convert_fusion
  179.8 29.3 %exchange_hidden.1 = bf16[32,32,512]{2,1,0:T(8,128)(2,1)} custom-call(bf16[32,32,512]{2,1,0:T(8,128)(2,1)} %bitcast.47), custom_call_target="tpu_custom_call" | custom-call | bytes 62914560 | tf_op jit(solution)/shard_map/exchange_hidden/pallas_call | solution.py:260
  209.1 1.7 reshape.155
  211.9 1.2 reshape.154
  213.5 2.3 %fusion.10 = (f32[1,512,8,128]{3,1,0,2:T(8,128)}, f32[1,512,8,128]{3,1,0,2:T(8,128)}) fusion(f32[2,512,8,128]{3,1,0,2:T(8,128)S(1)} %convert_bitcast_fusion), kind=kLoop, calls=%fused_computation.32 | loop fusion | bytes 8388608 | tf_op jit(solution)/shard_map/slice | solution.py:344
  215.8 1.9 copy.84
  217.8 1.8 copy.87
  219.6 1.9 copy.83
  221.5 1.8 copy.86
  (61 shorter events, 13.3 us)
Async XLA Ops:
  0.6 7.3 %copy-start.11 = (bf16[32,4096]{1,0:T(8,128)(2,1)S(1)}, bf16[32,4096]{1,0:T(8,128)(2,1)}, u32[]{:S(2)}) copy-start(bf16[32,4096]{1,0:T(8,128)(2,1)} %param.10) | copy-start | bytes 786436
  0.6 7.3 %copy-start.12 = (bf16[32,4096]{1,0:T(8,128)(2,1)S(1)}, bf16[32,4096]{1,0:T(8,128)(2,1)}, u32[]{:S(2)}) copy-start(bf16[32,4096]{1,0:T(8,128)(2,1)} %param.11) | copy-start | bytes 786436
  7.0 2.1 copy-start.8
  9.1 1.2 copy-start.9
  11.5 1.5 copy-start.10
  73.6 1.6 copy-start.2
  75.2 0.8 copy-start.3
  111.9 1.3 copy-start
  113.2 1.0 copy-start.1
  143.9 0.9 copy-start.4
  173.5 2.6 %copy-start.6 = (bf16[2,4,256,512]{3,2,1,0:T(8,128)(2,1)S(1)}, bf16[2,4,256,512]{3,2,1,0:T(8,128)(2,1)}, u32[]{:S(2)}) copy-start(bf16[2,4,256,512]{3,2,1,0:T(8,128)(2,1)} %get-tuple-element.22) | copy-start | bytes 6291460
  176.1 1.2 copy-start.7
  211.5 1.6 copy-start.5

commit v3 on v2

--- a/solution.py
+++ b/solution.py
@@ -21,12 +21,22 @@
     return lax.dot_general(a, b, dims, preferred_element_type=jnp.float32)
 
 
+def head_rows(qg_ref, first, per_part, which):
+    pieces = [
+        qg_ref[first + k, which, :, h * ATTN_WIDTH : (h + 1) * ATTN_WIDTH]
+        for k in range(per_part)
+        for h in range(GROUP)
+    ]
+    return jnp.concatenate(pieces, axis=0)
+
+
 def attention_kernel(
     blocks, tile_count, per_tile, counts, tiles, kv_ref, qg_ref, ld_ref, dkv_ref, dq_ref, dk_acc, dv_acc, dq_acc
 ):
     block = pl.program_id(0)
     per_part = per_tile // 2
-    wide = GROUP * TILE // per_tile
+    row_count = TILE // per_tile
+    wide = GROUP * row_count
 
     @pl.when(block == 0)
     def _():
@@ -43,8 +53,8 @@
         for part in range(2):
             rows = slice(part * 256, part * 256 + 256)
             first = tile * per_tile + part * per_part
-            q = qg_ref[pl.ds(first, per_part), 0].reshape(256, ATTN_WIDTH)
-            g = qg_ref[pl.ds(first, per_part), 1].reshape(256, ATTN_WIDTH)
+            q = head_rows(qg_ref, first, per_part, 0)
+            g = head_rows(qg_ref, first, per_part, 1)
             ld = jnp.concatenate([ld_ref[first + k] for k in range(per_part)], axis=1)
             lse, delta = ld[0:1], ld[1:2]
             prob = jnp.exp2(dot(keys, q, NT) * (SCALE * LOG2_E) - lse)
@@ -68,7 +78,10 @@
         def put(tile, carry):
             for k in range(per_tile):
                 piece = dq_acc[tile, :, k * wide : (k + 1) * wide] * SCALE
-                dq_ref[tile * per_tile + k] = piece.T.astype(dq_ref.dtype)
+                piece = piece.T.astype(dq_ref.dtype)
+                for h in range(GROUP):
+                    cols = slice(h * ATTN_WIDTH, (h + 1) * ATTN_WIDTH)
+                    dq_ref[tile * per_tile + k, :, cols] = piece[h * row_count : (h + 1) * row_count]
             return carry
 
         lax.fori_loop(0, tile_count, put, 0)
@@ -76,16 +89,15 @@
 
 def attention(counts, tiles, kv, qg, ld, out_dtype):
     blocks, _, span, width = kv.shape
-    sources, _, wide, _ = qg.shape
-    lanes = GROUP * TILE
-    per_tile = lanes // wide
+    sources, _, row_count, lanes = qg.shape
+    per_tile = TILE // row_count
     tile_count = sources // per_tile
     whole = lambda shape: pl.BlockSpec(shape, lambda b, *_: (0,) * len(shape))
     return pl.pallas_call(
         functools.partial(attention_kernel, blocks, tile_count, per_tile),
         out_shape=(
             jax.ShapeDtypeStruct(kv.shape, out_dtype),
-            jax.ShapeDtypeStruct((sources, wide, width), jnp.bfloat16),
+            jax.ShapeDtypeStruct((sources, row_count, lanes), jnp.bfloat16),
         ),
         grid_spec=pltpu.PrefetchScalarGridSpec(
             num_scalar_prefetch=2,
@@ -97,7 +109,7 @@
             ],
             out_specs=(
                 pl.BlockSpec((1, 2, span, width), lambda b, *_: (b, 0, 0, 0)),
-                whole((sources, wide, width)),
+                whole((sources, row_count, lanes)),
             ),
             scratch_shapes=[
                 pltpu.VMEM((span, width), jnp.float32),
@@ -269,6 +281,222 @@
     )(*arrays)
 
 
+def send_to(src, dst, send, recv, target):
+    return pltpu.make_async_remote_copy(
+        src_ref=src,
+        dst_ref=dst,
+        send_sem=send,
+        recv_sem=recv,
+        device_id={"psg": target},
+        device_id_type=pl.DeviceIdType.MESH,
+    )
+
+
+def inward_kernel(devices, slices, *refs):
+    q_ref, g_ref, ld_ref, k_ref, v_ref, qg_out, ld_out, kv_out = refs[:8]
+    in_send, in_recv, kv_send, kv_recv, ld_send, ld_recv, up_send, up_recv, down_send, down_recv, own = refs[8:]
+    layers = devices // slices
+    me = lax.axis_index("psg")
+    j, z = lax.rem(me, slices), me // slices
+    base = me - j
+    lanes, width = q_ref.shape[1] // slices, k_ref.shape[1] // slices
+    barrier = pltpu.get_barrier_semaphore()
+
+    def greet(r, c):
+        other = lax.rem(me + r, devices)
+        pl.semaphore_signal(barrier, inc=1, device_id={"psg": other}, device_id_type=pl.DeviceIdType.MESH)
+        return c
+
+    lax.fori_loop(1, devices, greet, 0)
+    pl.semaphore_wait(barrier, devices - 1)
+
+    def columns(ref, part, size):
+        return ref.at[:, pl.ds(pl.multiple_of(part * size, size), size)]
+
+    def inside(r):
+        other = lax.rem(j + r, slices)
+        return [
+            send_to(columns(ref, other, lanes), qg_out.at[me, i], in_send.at[i, r], in_recv.at[i, r], base + other)
+            for i, ref in enumerate((q_ref, g_ref))
+        ]
+
+    def passages(r):
+        other = lax.rem(j + r, slices)
+        return [
+            send_to(columns(ref, other, width), kv_out.at[j, i], kv_send.at[i, r], kv_recv.at[i, r], base + other)
+            for i, ref in enumerate((k_ref, v_ref))
+        ]
+
+    def small(r):
+        other = lax.rem(me + r, devices)
+        return send_to(ld_ref.at[lax.rem(other, slices)], ld_out.at[me], ld_send.at[r], ld_recv.at[r], other)
+
+    def hop(sent, r, up):
+        layer = z - sent if up else z + sent
+        source = layer * slices + lax.rem(j - r + slices, slices)
+        ref = qg_out.at[source]
+        if up:
+            return send_to(ref, ref, up_send.at[sent, r], up_recv.at[sent, r], me + slices)
+        return send_to(ref, ref, down_send.at[sent, r], down_recv.at[sent, r], me - slices)
+
+    def hop_here(sent, r, up):
+        layer = z - sent - 1 if up else z + sent + 1
+        source = layer * slices + lax.rem(j - r + slices, slices)
+        ref = qg_out.at[source]
+        if up:
+            return send_to(ref, ref, up_send.at[sent, r], up_recv.at[sent, r], lax.rem(me + 1, devices))
+        return send_to(ref, ref, down_send.at[sent, r], down_recv.at[sent, r], lax.rem(me + 1, devices))
+
+    kept = [
+        pltpu.make_async_copy(columns(q_ref, j, lanes), qg_out.at[me, 0], own.at[0]),
+        pltpu.make_async_copy(columns(g_ref, j, lanes), qg_out.at[me, 1], own.at[1]),
+        pltpu.make_async_copy(columns(k_ref, j, width), kv_out.at[j, 0], own.at[2]),
+        pltpu.make_async_copy(columns(v_ref, j, width), kv_out.at[j, 1], own.at[3]),
+        pltpu.make_async_copy(ld_ref.at[j], ld_out.at[me], own.at[4]),
+    ]
+    for copy in kept:
+        copy.start()
+    for r in range(1, slices):
+        for copy in inside(r):
+            copy.start()
+    for copy in kept:
+        copy.wait()
+
+    def forward(sent, r):
+        @pl.when((z < layers - 1) & (z >= sent))
+        def _():
+            hop(sent, r, True).start()
+
+        @pl.when((z > 0) & (z + sent < layers))
+        def _():
+            hop(sent, r, False).start()
+
+    forward(0, 0)
+
+    def first(r, c):
+        for copy in inside(r):
+            copy.wait_recv()
+        forward(0, r)
+        return c
+
+    lax.fori_loop(1, slices, first, 0)
+    for r in range(1, slices):
+        for copy in passages(r):
+            copy.start()
+    lax.fori_loop(1, devices, lambda r, c: (small(r).start(), c)[1], 0)
+
+    def later(n, c):
+        sent, r = n // slices, lax.rem(n, slices)
+
+        @pl.when(z > sent)
+        def _():
+            hop_here(sent, r, True).wait_recv()
+
+        @pl.when((z > sent) & (z < layers - 1))
+        def _():
+            hop(sent + 1, r, True).start()
+
+        @pl.when(z + sent + 1 < layers)
+        def _():
+            hop_here(sent, r, False).wait_recv()
+
+        @pl.when((z + sent + 1 < layers) & (z > 0))
+        def _():
+            hop(sent + 1, r, False).start()
+
+        return c
+
+    lax.fori_loop(0, (layers - 1) * slices, later, 0)
+
+    for r in range(1, slices):
+        for copy in inside(r):
+            copy.wait_send()
+        for copy in passages(r):
+            copy.wait()
+    lax.fori_loop(1, devices, lambda r, c: (small(r).wait(), c)[1], 0)
+
+    def ended(n, c):
+        sent, r = n // slices, lax.rem(n, slices)
+
+        @pl.when((z < layers - 1) & (z >= sent))
+        def _():
+            hop(sent, r, True).wait_send()
+
+        @pl.when((z > 0) & (z + sent < layers))
+        def _():
+            hop(sent, r, False).wait_send()
+
+        return c
+
+    lax.fori_loop(0, (layers - 1) * slices, ended, 0)
+
+
+def inward(devices, slices, queries, grad_out, ld, keys, values):
+    layers = devices // slices
+    row_count, columns = queries.shape
+    span = keys.shape[0]
+    dma = pltpu.SemaphoreType.DMA
+    anywhere = pl.BlockSpec(memory_space=pl.ANY)
+    return pl.pallas_call(
+        functools.partial(inward_kernel, devices, slices),
+        out_shape=(
+            jax.ShapeDtypeStruct((devices, 2, row_count, columns // slices), queries.dtype),
+            jax.ShapeDtypeStruct((devices,) + ld.shape[1:], ld.dtype),
+            jax.ShapeDtypeStruct((slices, 2, span, keys.shape[1] // slices), keys.dtype),
+        ),
+        in_specs=[anywhere] * 5,
+        out_specs=(anywhere,) * 3,
+        scratch_shapes=[dma((2, slices))] * 4
+        + [dma((devices,))] * 2
+        + [dma((layers, slices))] * 4
+        + [dma((5,))],
+        compiler_params=pltpu.CompilerParams(collective_id=0, has_side_effects=True),
+        cost_estimate=pl.CostEstimate(flops=0, bytes_accessed=60 * 2**20, transcendentals=0),
+        name="exchange_in",
+    )(queries, grad_out, ld, keys, values)
+
+
+def finish_kernel(slices, dkv_ref, hidden_ref, dk_ref, dv_ref, out_ref):
+    step = pl.program_id(0)
+    dk_ref[...] = dkv_ref[0, 0].astype(jnp.float32)
+    dv_ref[...] = dkv_ref[0, 1].astype(jnp.float32)
+    quads = slices // 2
+    width = hidden_ref.shape[-1] // quads
+    layers = hidden_ref.shape[0]
+
+    @pl.when(step < 2 * layers)
+    def _():
+        z, parity = step // 2, lax.rem(step, 2)
+        total = hidden_ref[z, 0, parity].astype(jnp.float32)
+        for k in range(1, quads):
+            total += hidden_ref[z, k, parity].astype(jnp.float32)
+        for k in range(quads):
+            first = (z * slices + 2 * k + parity) * width
+            out_ref[:, pl.ds(pl.multiple_of(first, width), width)] = total[:, k * width : (k + 1) * width]
+
+
+def finish(slices, dkv, hidden):
+    _, _, span, width = dkv.shape
+    layers, quads, _, row_count, part = hidden.shape
+    out = jax.ShapeDtypeStruct((span, slices * width), jnp.float32)
+    return pl.pallas_call(
+        functools.partial(finish_kernel, slices),
+        out_shape=(out, out, jax.ShapeDtypeStruct((row_count, layers * 2 * part), jnp.float32)),
+        grid=(max(slices, 2 * layers),),
+        in_specs=[
+            pl.BlockSpec((1, 2, span, width), lambda s: (jnp.minimum(s, slices - 1), 0, 0, 0)),
+            pl.BlockSpec(hidden.shape, lambda s: (0, 0, 0, 0, 0)),
+        ],
+        out_specs=(
+            pl.BlockSpec((span, width), lambda s: (0, jnp.minimum(s, slices - 1))),
+            pl.BlockSpec((span, width), lambda s: (0, jnp.minimum(s, slices - 1))),
+            pl.BlockSpec((row_count, layers * 2 * part), lambda s: (0, 0)),
+        ),
+        cost_estimate=pl.CostEstimate(flops=0, bytes_accessed=8 * 2**20, transcendentals=0),
+        name="finish",
+    )(dkv, hidden)
+
+
 def on_device(queries, grad_out, attn_out, log_sum, keys, values, proj_weight, attend, qlen):
     row_count, columns = queries.shape
     head_count = log_sum.shape[0]
@@ -282,16 +510,15 @@
     tile_count = devices * row_count // TILE
     run = functools.partial(exchange, devices=devices, slices=slices)
 
-    kv = jnp.stack([keys, values]).reshape(2, span, slices, ATTN_WIDTH).transpose(2, 0, 1, 3)
-    qg = jnp.stack([queries, grad_out]).reshape(2, row_count, slices, GROUP, ATTN_WIDTH)
-    qg = qg.transpose(2, 0, 3, 1, 4).reshape(slices, 2, wide, ATTN_WIDTH)
     products = grad_out.astype(jnp.float32) * attn_out.astype(jnp.float32)
     delta = jnp.sum(products.reshape(row_count, head_count, ATTN_WIDTH), axis=2).T
     ld = jnp.stack([log_sum * LOG2_E, delta])
     ld = ld.reshape(2, slices, wide).transpose(1, 0, 2)
     if slices > 1:
-        qg, ld, kv = run("exchange_in", 0, parts=[("cast", qg), ("cast", ld), ("layer", kv)])
+        qg, ld, kv = inward(devices, slices, queries, grad_out, ld, keys, values)
     else:
+        kv = jnp.stack([keys, values])[None]
+        qg = jnp.stack([queries, grad_out])[None]
         qg, ld = run("exchange_in", 0, parts=[("cast", qg), ("cast", ld)])
 
     block_ids = (me // slices) * slices + jnp.arange(slices, dtype=jnp.int32)
@@ -308,14 +535,13 @@
     out_dtype = jnp.bfloat16 if slices > 1 else jnp.float32
     dkv, dq = attention(counts, tiles, kv, qg, ld, out_dtype)
 
-    dq = dq.reshape(layers, slices, wide, ATTN_WIDTH)
+    dq = dq.reshape(layers, slices, row_count, lanes)
     if slices > 1:
         dq, dkv = run("exchange_terms", 1, parts=[("z", dq), ("layer", dkv)])
     else:
         (dq,) = run("exchange_terms", 1, parts=[("all", dq)])
     summed = jnp.sum(dq.astype(jnp.float32), axis=0)
-    low = summed.astype(jnp.bfloat16).reshape(slices, GROUP, row_count, ATTN_WIDTH)
-    low = low.transpose(0, 2, 1, 3).reshape(slices * row_count, lanes)
+    low = summed.astype(jnp.bfloat16).reshape(slices * row_count, lanes)
 
     out_columns = proj_weight.shape[0]
     if slices > 1:
@@ -328,20 +554,17 @@
         hidden = dot(low[0], weight[:, :lanes], NT) + dot(low[1], weight[:, lanes:], NT)
         hidden = hidden.astype(jnp.bfloat16).reshape(devices, row_count, slices // 2 * out_columns)
         (hidden,) = run("exchange_hidden", 3, parts=[("all", hidden)])
-        hidden = hidden.reshape(layers, slices // 2, 2, row_count, slices // 2, out_columns)
-        hidden = jnp.sum(hidden.astype(jnp.float32), axis=1)
-        hidden = hidden.transpose(2, 0, 3, 1, 4).reshape(row_count, devices * out_columns)
+        hidden = hidden.reshape(layers, slices // 2, 2, row_count, slices // 2 * out_columns)
+        grad_keys, grad_values, hidden = finish(slices, dkv, hidden)
     else:
         all_low = lax.all_gather(low, "psg", axis=0, tiled=True)
         hidden = dot(all_low, proj_weight, NT)
         hidden = lax.all_to_all(hidden.reshape(devices, row_count, out_columns), "psg", 0, 0)
         hidden = hidden.transpose(1, 0, 2).reshape(row_count, devices * out_columns)
+        grad_keys, grad_values = dkv[0, 0], dkv[0, 1]
     grad_hidden = lax.psum(hidden, "qry")
-
-    grad_query = summed.reshape(slices, GROUP, row_count, ATTN_WIDTH)
-    grad_query = grad_query.transpose(2, 0, 1, 3).reshape(row_count, columns)
-    dkv = dkv.astype(jnp.float32).transpose(1, 2, 0, 3).reshape(2, span, slices * ATTN_WIDTH)
-    return (grad_query, dkv[0], dkv[1], grad_hidden)
+    grad_query = summed.transpose(1, 0, 2).reshape(row_count, columns)
+    return (grad_query, grad_keys, grad_values, grad_hidden)
 
 
 def solution(mesh):

time: 221 us -> 195 us (0.88); the launches traced: 223 us -> 191 us
  local copies, waits for them, and re-layouts: 30.6 us -> 11.7 us
  Pallas kernels: 181 us -> 170 us
  other arithmetic: 8.59 us -> 6.15 us
    pallas_call x4 -> x3, Pallas kernels: 145 us -> 85.5 us  [exchange(): pl.pallas_call(functools.partial(exchange_kernel, kinds, devices, slices,...]
    pallas_call x0 -> x2, Pallas kernels: none -> 57.6 us  [the longest x1 50.9 us: inward(): pl.pallas_call(functools.partial(inward_kernel, devices, slices), out_sha...]
    pallas_call x1, Pallas kernels: 35.9 us -> 27.1 us  [attention(): pl.pallas_call(functools.partial(attention_kernel, blocks, tile_count, pe...]
    unnamed x33 -> x18, local copies, waits for them, and re-layouts: 11.9 us -> 5.48 us
    slice x3 -> x0, local copies, waits for them, and re-layouts: 6.15 us -> none  [on_device(): return (grad_query, dkv[0], dkv[1], grad_hidden)]
    another operation x6 -> x0, local copies, waits for them, and re-layouts: 3.77 us -> none  [the longest x4 2.44 us: on_device(): jnp.stack([queries, grad_out])]
where the time goes in v3:
time: 195 us; the launch traced here: 191 us
  Pallas kernels  170 us (87%)
  local copies, waits for them, and re-layouts  11.7 us (6%)
  other arithmetic  6.15 us (3%)
  matrix products  2.46 us (1%)
    pallas_call x3, Pallas kernels, exchange(): pl.pallas_call(functools.partial(exchange_kernel, kinds, devices, slices,...  85.5 us
    pallas_call x1, Pallas kernels, inward(): pl.pallas_call(functools.partial(inward_kernel, devices, slices), out_sha...  50.9 us
    pallas_call x1, Pallas kernels, attention(): pl.pallas_call(functools.partial(attention_kernel, blocks, tile_count, pe...  27.1 us
    pallas_call x1, Pallas kernels, finish(): pl.pallas_call(functools.partial(finish_kernel, slices), out_shape=(out,...  6.65 us
    unnamed x18, local copies, waits for them, and re-layouts  5.48 us

profile of v3, /device:TPU:15, one launch (start us, length us, event | category | flops | bytes accessed | tf_op | source)
XLA Modules:
  0.0 191.3 jit_solution(1901363447856205085)
XLA Ops:
  0.6 0.7 fusion.6
  1.4 0.9 compare_reduce_fusion
  2.4 0.7 broadcast_in_dim.26
  3.5 0.2 select_reduce_fusion.tiles
  3.7 1.1 multiply_bitcast_fusion
  5.4 0.6 maximum_bitcast_fusion.refs_2_
  6.0 50.9 %exchange_in.1 = (bf16[32,2,32,512]{3,2,1,0:T(8,128)(2,1)}, f32[32,2,128]{2,1,0:T(2,128)}, bf16[8,2,512,128]{3,2,1,0:T(8,128)(2,1)}) custom-call(bf16[32,4096]{1,0:T(8,128)(2,1)} %refs_0_.1, bf16[32,4096]{1,0:T(8,128)(2,1)} %refs_1_.1, f32[8,2,128]{2,1,0:T(2,128)} %maximum_bitcast_fusion.refs_2_, bf16[512,1024]{1,0:T(8,128)(2,1)} %refs_3_.1, ...), custom_call_target="tpu_custom_call" | custom-call | bytes 62914560 | tf_op jit(solution)/shard_map/exchange_in/pallas_call | solution.py:440
  56.9 1.6 copy-done.2
  58.5 0.8 copy-done.3
  59.3 27.1 %attention.1 = (bf16[8,2,512,128]{3,2,1,0:T(8,128)(2,1)S(1)}, bf16[32,32,512]{2,1,0:T(8,128)(2,1)S(1)}) custom-call(s32[8]{0:T(128)S(1)} %fusion.4.counts, s32[8,8]{1,0:T(8,128)S(1)} %select_reduce_fusion.tiles, bf16[8,2,512,128]{3,2,1,0:T(8,128)(2,1)S(1)} %copy-done.2, bf16[32,2,32,512]{3,2,1,0:T(8,128)(2,1)} %get-tuple-element.18.qg_ref, ...), custom_call_target="tpu_custom_call" | custom-call | flops 10737418240 | bytes 16777216 | tf_op jit(solution)/shard_map/attention/pallas_call | solution.py:96
  86.4 1.3 copy-done
  87.7 1.0 copy-done.1
  88.7 27.1 %exchange_terms.1 = (bf16[4,8,32,512]{3,2,1,0:T(8,128)(2,1)}, bf16[8,2,512,128]{3,2,1,0:T(8,128)(2,1)}) custom-call(bf16[4,8,32,512]{3,2,1,0:T(8,128)(2,1)} %bitcast.22, bf16[8,2,512,128]{3,2,1,0:T(8,128)(2,1)} %copy-done), custom_call_target="tpu_custom_call" | custom-call | bytes 62914560 | tf_op jit(solution)/shard_map/exchange_terms/pallas_call | solution.py:272
  115.8 1.4 convert_reduce_fusion.refs_0_
  117.3 0.7 copy.29
  118.0 1.3 copy.30
  119.3 0.7 convert_element_type.35
  120.0 28.7 %exchange_rows.1 = (f32[8,32,512]{2,1,0:T(8,128)}, bf16[4,128,1024]{2,1,0:T(8,128)(2,1)}, bf16[2,4,256,512]{3,2,1,0:T(8,128)(2,1)}) custom-call(f32[8,32,512]{2,1,0:T(8,128)} %copy-done.4, bf16[4,128,1024]{2,1,0:T(8,128)(2,1)} %bitcast.24, bf16[256,512]{1,0:T(8,128)(2,1)} %bitcast.32), custom_call_target="tpu_custom_call" | custom-call | bytes 62914560 | tf_op jit(solution)/shard_map/exchange_rows/pallas_call | solution.py:272
  148.7 1.9 copy.32
  150.6 1.8 fusion.10
  152.4 0.7 fusion.1
  153.2 1.7 add_convert_fusion
  154.9 29.7 %exchange_hidden.1 = bf16[32,32,512]{2,1,0:T(8,128)(2,1)} custom-call(bf16[32,32,512]{2,1,0:T(8,128)(2,1)} %bitcast.27), custom_call_target="tpu_custom_call" | custom-call | bytes 62914560 | tf_op jit(solution)/shard_map/exchange_hidden/pallas_call | solution.py:272
  184.6 6.7 %finish.1 = (f32[512,1024]{1,0:T(8,128)}, f32[512,1024]{1,0:T(8,128)}, f32[32,4096]{1,0:T(8,128)}) custom-call(bf16[8,2,512,128]{3,2,1,0:T(8,128)(2,1)} %get-tuple-element.24.dkv_ref, bf16[4,4,2,32,512]{4,3,2,1,0:T(8,128)(2,1)} %bitcast.23), custom_call_target="tpu_custom_call" | custom-call | bytes 8388608 | tf_op jit(solution)/shard_map/finish/pallas_call | solution.py:482
  (29 shorter events, 1.1 us)
Async XLA Ops:
  0.6 4.6 %copy-start.7 = (f32[32,32]{1,0:T(8,128)S(1)}, f32[32,32]{1,0:T(8,128)}, u32[]{:S(2)}) copy-start(f32[32,32]{1,0:T(8,128)} %param.12) | copy-start | bytes 12292
  56.9 1.6 copy-start.2
  58.5 0.8 copy-start.3
  86.4 1.3 copy-start
  87.7 1.0 copy-start.1
  88.7 28.6 %copy-start.6 = (bf16[128,4096]{1,0:T(8,128)(2,1)S(1)}, bf16[128,4096]{1,0:T(8,128)(2,1)}, u32[]{:S(2)}) copy-start(bf16[128,4096]{1,0:T(8,128)(2,1)} %param.15) | copy-start | bytes 3145732
  117.3 2.0 %copy-start.4 = (f32[8,32,512]{2,1,0:T(8,128)}, f32[8,32,512]{2,1,0:T(8,128)S(1)}, u32[]{:S(2)}) copy-start(f32[8,32,512]{2,1,0:T(8,128)S(1)} %convert_reduce_fusion.refs_0_) | copy-start | bytes 1572868
  150.6 1.9 copy-start.5
